TPU v7x, 256 devices: a whole 4x4x8 slice. The times are simulated.
256 devices in a mesh: blk: 32 (over x_lo, z, core), grp: 8 (over x_hi, y).
Axes of the slice: x: 4 (x_hi: 2, x_lo: 2; x = x_hi * 2 + x_lo), y: 4, z: 8, core: 2. Of those that a mesh axis runs over, the one named last changes fastest.
Arguments:
- spectra: bfloat16 [2, 128, 640, 4096], P(None, 'grp', None, 'blk'), may hold values from -6 to 6
- pattern: int32 [32, 32], replicated, may hold values from 0 to 1, as said below
- slot_of_pair: int32 [32, 32], replicated, may hold values from 0 to 7, as said below
Outputs:
- stacks: bfloat16 [8, 512, 4, 4096], P('grp', None, None, 'blk')
Inputs may be any that keep to these rules, and one draw needn't show every extreme that they name: `pattern`: every block pairs with itself and with the blocks next to it; each column j holds at most 8 ones, and some column exactly 8. `slot_of_pair`: within a column j the pairs with pattern 1 have distinct slots; slots g * 1 to (g + 1) - 1 belong to owner g of the grp axis; in some column every slot is used. Entries where pattern is 0 carry no meaning.
All inputs are finite; a program needn't handle non-finite values.
Results may differ from a plain program's by a relative error of at most 0.0055.
Values may be sent and summed in bfloat16 or wider, within the bound.
A program may use at most 128 MiB of HBM per device.

v0:
```python
import math

import jax
import jax.numpy as jnp
from jax import lax
from jax.sharding import PartitionSpec as P

F = 640
LAGS = 512
VS = 4
PAIRS_MAX = 8


def share_table(count, lag_count, windows, repeats):
    freq_bins = jnp.arange(count, dtype=jnp.int32)
    shifts = jnp.arange(lag_count, dtype=jnp.int32) - lag_count // 2
    phases = shifts[:, None] * freq_bins[None, :] % (2 * F)
    angles = math.pi / F * phases.astype(jnp.float32)
    factor = 1.0 / math.sqrt(2.0 * windows * F)
    rows = jnp.concatenate([jnp.cos(angles), -jnp.sin(angles)], axis=1) * factor
    return jnp.tile(rows, (1, repeats)).astype(jnp.bfloat16)


def cross_spectra(sources, receivers):
    turned = jnp.stack([sources[1], -sources[0]])
    real_part = jnp.einsum(
        "pgwsf,pgwfc->gfsc", sources, receivers, preferred_element_type=jnp.float32
    )
    imag_part = jnp.einsum(
        "pgwsf,pgwfc->gfsc", turned, receivers, preferred_element_type=jnp.float32
    )
    crossed = jnp.stack([real_part, imag_part], axis=1).astype(jnp.bfloat16)
    segments = crossed.shape[0]
    return crossed.reshape(segments * 2 * crossed.shape[2], crossed.shape[3] * crossed.shape[4])


def make_visitor(pattern, slot_of_pair, column, receivers, transform):
    segments = receivers.shape[1]
    win_count = receivers.shape[2]
    freq_count = receivers.shape[3]
    channels = receivers.shape[4]
    zero_index = jnp.zeros((), jnp.int32)

    def add_pair(buffer, source_block, sources):
        active = pattern[source_block, column] > 0
        target_slot = slot_of_pair[source_block, column]

        def compute(buffer):
            crossed = cross_spectra(sources, receivers)
            lagged = jnp.dot(transform, crossed, preferred_element_type=jnp.float32)
            lagged = lagged.reshape(1, LAGS, VS, channels)
            return lax.dynamic_update_slice(
                buffer, lagged, (target_slot, zero_index, zero_index, zero_index)
            )

        return lax.cond(active, compute, lambda kept: kept, buffer)

    def visit_all(buffer, portion, offset):

        def visit(number, buffer):
            sources = lax.dynamic_index_in_dim(portion, number, 0, keepdims=False)
            sources = sources.reshape(2, segments, win_count, VS, freq_count)
            return add_pair(buffer, number, sources)

        return lax.fori_loop(0, portion.shape[0], visit, buffer)

    return visit_all


def per_device(spectra, pattern, slot_of_pair):
    groups = lax.axis_size("grp")
    column = lax.axis_index("blk")
    win_count = spectra.shape[1]
    freq_count = spectra.shape[2]
    channels = spectra.shape[3]
    empty = jnp.zeros((PAIRS_MAX, LAGS, VS, channels), jnp.float32)
    own_sources = jnp.transpose(spectra[:, :, :, :VS], (0, 1, 3, 2))[None]
    transform = share_table(freq_count, LAGS, win_count * groups, 1)
    receivers = spectra.reshape(2, 1, win_count, freq_count, channels)
    visit_all = make_visitor(pattern, slot_of_pair, column, receivers, transform)
    buffer = visit_all(empty, lax.all_gather(own_sources, "blk", axis=0, tiled=True), jnp.int32(0))
    summed = lax.psum_scatter(buffer, "grp", scatter_dimension=0, tiled=True)
    return summed.astype(jnp.bfloat16)


def solution(mesh):
    return jax.shard_map(
        per_device,
        mesh=mesh,
        in_specs=(P(None, "grp", None, "blk"), P(), P()),
        out_specs=P("grp", None, None, "blk"),
        check_vma=False,
    )
```

profile of v0, /device:TPU:1, one launch (start us, length us, event | category | flops | bytes accessed | tf_op | source)
XLA Modules:
  0.0 438.6 jit_solution(7539386758850189206)
XLA Ops:
  6.5 4.9 %copy.20 = bf16[2,16,640,4]{2,1,3,0:T(8,128)(2,1)} copy(bf16[2,16,640,4]{3,2,1,0:T(8,128)(2,1)} %bitcast.66) | data formatting | bytes 327680
  11.5 8.2 %copy.27 = bf16[2,16,640,128]{3,1,0,2:T(8,128)(2,1)} copy(bf16[2,16,640,128]{3,2,1,0:T(8,128)(2,1)} %param.7) | data formatting | bytes 10485760 | tf_op args[0]
  19.7 5.4 %fusion.36 = (f32[512,640]{1,0:T(8,128)S(1)}, f32[512,640]{1,0:T(8,128)S(1)}) fusion(s32[512]{0:T(512)S(1)} %iota_add_fusion), kind=kLoop, calls=%fused_computation.31 | loop fusion | flops 3276800 | bytes 2623488 | tf_op jit(solution)/shard_map/cos | solution.py:20
  25.3 58.8 %all-gather.3.cloned.1.call-done = bf16[64,16,4,640]{3,1,2,0:T(8,128)(2,1)} async-done(((bf16[2,16,4,640]{3,1,2,0:T(8,128)(2,1)}), bf16[64,16,4,640]{3,1,2,0:T(8,128)(2,1)}) %all-gather.3.cloned.1.call-update) | async-done | bytes 5242896 | tf_op jit(solution)/shard_map/all_gather | solution.py:81
  84.1 4.3 broadcast_in_dim.8
  88.4 120.1 %while.18 = (s32[]{:T(128)}, f32[8,512,4,128]{1,3,2,0:T(8,128)}, s32[32,32]{1,0:T(8,128)}, s32[]{:T(128)}, bf16[32,2,16,4,640]{4,2,3,1,0:T(8,128)(2,1)}, /*index...) while((s32[]{:T(128)}, f32[8,512,4,128]{1,3,2,0:T(8,128)}, ...), condition=%wide.region_3.4_spmd, body=%wide.region_0.3_spmd.sunk | while | flops 714465280 | bytes 22151432 | solution.py:65
  90.3 19.2 %conditional.2 = (f32[8,512,4,128]{1,3,2,0:T(8,128)}) conditional(s32[]{:T(128)} %bitcast.63, f32[8,512,4,128]{1,3,2,0:T(8,128)} %get-tuple-element.355, (bf16[32,2,16,4,640]{4,2,3,1,0:T(8,128)(2,1)}, s32[]{:T(128)}, bf16[2,1,16,640,128]{4,2,0,3,1:T(8,128)(2,1)}, bf16[512,1280]{1,0:T(8,128)(2,1)S(1)}, s32[32,32]{1,0:T(8,128)}, /*index=5*/s32[]{:T(128)}, ...), branch_computations={%region_1.1_spmd, %region_2.2_spmd} | conditional | flops 714465280 | bytes 22151248 | solution.py:56
  92.4 4.5 %fusion.26 = bf16[1,1,640,4,128]{4,3,2,1,0:T(4,128)(2,1)S(1)} fusion(bf16[2,1,16,640,128]{4,2,0,3,1:T(8,128)(2,1)} %get-tuple-element.252, bf16[2,1,16,4,640]{2,3,0,4,1:T(4,128)(2,1)S(1)} %copy.13), kind=kOutput, calls=%fused_computation.15 | convolution fusion | flops 21299200 | bytes 6062080 | tf_op jit(solution)/shard_map/while/body/eval_jaxpr/cond/branch_1_fun/pgwsf,pgwfc->gfsc/dot_general | solution.py:29
  98.9 4.5 %fusion.21 = bf16[1,1,640,4,128]{4,3,2,1,0:T(4,128)(2,1)S(1)} fusion(bf16[2,1,16,640,128]{4,2,0,3,1:T(8,128)(2,1)} %get-tuple-element.252, bf16[1,2,16,4,640]{2,3,1,4,0:T(4,128)(2,1)S(1)} %copy.12), kind=kOutput, calls=%fused_computation.14 | convolution fusion | flops 21299200 | bytes 6062080 | tf_op jit(solution)/shard_map/while/body/eval_jaxpr/cond/branch_1_fun/pgwsf,pgwfc->gfsc/dot_general | solution.py:26
  105.2 1.3 dynamic_slice.32
  111.4 19.2 %conditional.2 = (f32[8,512,4,128]{1,3,2,0:T(8,128)}) conditional(s32[]{:T(128)} %bitcast.63, f32[8,512,4,128]{1,3,2,0:T(8,128)} %get-tuple-element.355, (bf16[32,2,16,4,640]{4,2,3,1,0:T(8,128)(2,1)}, s32[]{:T(128)}, bf16[2,1,16,640,128]{4,2,0,3,1:T(8,128)(2,1)}, bf16[512,1280]{1,0:T(8,128)(2,1)S(1)}, s32[32,32]{1,0:T(8,128)}, /*index=5*/s32[]{:T(128)}, ...), branch_computations={%region_1.1_spmd, %region_2.2_spmd} | conditional | flops 714465280 | bytes 22151248 | solution.py:56
  113.5 4.5 %fusion.26 = bf16[1,1,640,4,128]{4,3,2,1,0:T(4,128)(2,1)S(1)} fusion(bf16[2,1,16,640,128]{4,2,0,3,1:T(8,128)(2,1)} %get-tuple-element.252, bf16[2,1,16,4,640]{2,3,0,4,1:T(4,128)(2,1)S(1)} %copy.13), kind=kOutput, calls=%fused_computation.15 | convolution fusion | flops 21299200 | bytes 6062080 | tf_op jit(solution)/shard_map/while/body/eval_jaxpr/cond/branch_1_fun/pgwsf,pgwfc->gfsc/dot_general | solution.py:29
  120.0 4.5 %fusion.21 = bf16[1,1,640,4,128]{4,3,2,1,0:T(4,128)(2,1)S(1)} fusion(bf16[2,1,16,640,128]{4,2,0,3,1:T(8,128)(2,1)} %get-tuple-element.252, bf16[1,2,16,4,640]{2,3,1,4,0:T(4,128)(2,1)S(1)} %copy.12), kind=kOutput, calls=%fused_computation.14 | convolution fusion | flops 21299200 | bytes 6062080 | tf_op jit(solution)/shard_map/while/body/eval_jaxpr/cond/branch_1_fun/pgwsf,pgwfc->gfsc/dot_general | solution.py:26
  126.3 1.3 dynamic_slice.32
  132.5 19.1 %conditional.2 = (f32[8,512,4,128]{1,3,2,0:T(8,128)}) conditional(s32[]{:T(128)} %bitcast.63, f32[8,512,4,128]{1,3,2,0:T(8,128)} %get-tuple-element.355, (bf16[32,2,16,4,640]{4,2,3,1,0:T(8,128)(2,1)}, s32[]{:T(128)}, bf16[2,1,16,640,128]{4,2,0,3,1:T(8,128)(2,1)}, bf16[512,1280]{1,0:T(8,128)(2,1)S(1)}, s32[32,32]{1,0:T(8,128)}, /*index=5*/s32[]{:T(128)}, ...), branch_computations={%region_1.1_spmd, %region_2.2_spmd} | conditional | flops 714465280 | bytes 22151248 | solution.py:56
  134.5 4.5 %fusion.26 = bf16[1,1,640,4,128]{4,3,2,1,0:T(4,128)(2,1)S(1)} fusion(bf16[2,1,16,640,128]{4,2,0,3,1:T(8,128)(2,1)} %get-tuple-element.252, bf16[2,1,16,4,640]{2,3,0,4,1:T(4,128)(2,1)S(1)} %copy.13), kind=kOutput, calls=%fused_computation.15 | convolution fusion | flops 21299200 | bytes 6062080 | tf_op jit(solution)/shard_map/while/body/eval_jaxpr/cond/branch_1_fun/pgwsf,pgwfc->gfsc/dot_general | solution.py:29
  141.0 4.5 %fusion.21 = bf16[1,1,640,4,128]{4,3,2,1,0:T(4,128)(2,1)S(1)} fusion(bf16[2,1,16,640,128]{4,2,0,3,1:T(8,128)(2,1)} %get-tuple-element.252, bf16[1,2,16,4,640]{2,3,1,4,0:T(4,128)(2,1)S(1)} %copy.12), kind=kOutput, calls=%fused_computation.14 | convolution fusion | flops 21299200 | bytes 6062080 | tf_op jit(solution)/shard_map/while/body/eval_jaxpr/cond/branch_1_fun/pgwsf,pgwfc->gfsc/dot_general | solution.py:26
  147.4 1.3 dynamic_slice.32
  157.5 1.3 dynamic_slice.36
  159.5 1.3 dynamic_slice.36
  161.4 1.3 dynamic_slice.36
  163.4 1.3 dynamic_slice.36
  165.4 1.3 dynamic_slice.36
  167.3 1.3 dynamic_slice.36
  169.3 1.3 dynamic_slice.36
  171.3 1.3 dynamic_slice.36
  177.1 1.3 dynamic_slice.36
  179.1 1.3 dynamic_slice.36
  181.1 1.3 dynamic_slice.36
  208.5 9.1 %copy.16 = f32[8,512,4,128]{3,1,2,0:T(8,128)} copy(f32[8,512,4,128]{1,3,2,0:T(8,128)} %get-tuple-element.266) | data formatting | bytes 16777216 | tf_op jit(solution)/shard_map/while | solution.py:65
  217.7 211.5 %reduce-scatter.2.cloned.1.call-done = f32[1,512,4,128]{3,1,2,0:T(8,128)} async-done(((f32[8,512,4,128]{3,1,2,0:T(8,128)}), f32[1,512,4,128]{3,1,2,0:T(8,128)}) %reduce-scatter.2.cloned.1.call-update) | async-done | bytes 1048592 | tf_op jit(solution)/shard_map/reduce_scatter | solution.py:82
  429.2 1.3 convert_element_type.34
  (81 shorter events, 49.3 us)
Async XLA Ops:
  6.5 77.6 %all-gather.3.cloned.1.call-start = ((), (), s32[]{:S(2)}) async-start(), calls=%async_computation.2 | async-start | bytes 5406720 | tf_op jit(solution)/shard_map/all_gather | solution.py:81
  11.4 417.8 %reduce-scatter.2.cloned.1.call-start = ((), (), s32[]{:S(2)}) async-start(), calls=%async_computation.1 | async-start | bytes 9437184 | tf_op jit(solution)/shard_map/reduce_scatter | solution.py:82
Sparse Core Ops, SparseCore 0:
  11.6 72.4 all-gather.2
  217.8 211.3 reduce-scatter.1
where the time goes:
time: 442 us; the launch traced here: 439 us
  waiting for transfers between devices  270 us (61%)
  local copies, waits for them, and re-layouts  84.7 us (19%)
  matrix products  29.6 us (7%)
  loops' own time  27.7 us (6%)
  between operations  13.4 us (3%)
  other arithmetic  12.6 us (3%)
    reduce_scatter x1, waiting for transfers between devices, per_device(): summed = lax.psum_scatter(buffer, 'grp', scatter_dimension=0, tiled=True)  212 us
    all_gather x1, waiting for transfers between devices, per_device(): lax.all_gather(own_sources, 'blk', axis=0, tiled=True)  58.8 us
    dynamic_slice x32, local copies, waits for them, and re-layouts, add_pair(): active = pattern[source_block, column] > 0  40.8 us
    another operation x1, loops' own time, visit_all(): return lax.fori_loop(0, portion.shape[0], visit, buffer)  21.6 us
    dot_general x3, matrix products, cross_spectra(): jnp.einsum('pgwsf,pgwfc->gfsc', sources, receivers, preferred_element_typ...  13.5 us
    dot_general x3, matrix products, cross_spectra(): jnp.einsum('pgwsf,pgwfc->gfsc', turned, receivers, preferred_element_type...  13.5 us
    unnamed x2, local copies, waits for them, and re-layouts  13 us
    while x1, local copies, waits for them, and re-layouts, visit_all(): return lax.fori_loop(0, portion.shape[0], visit, buffer)  9.12 us
  transfers between devices with their start and end apart: 2, of which 2 were waited for; matrix products, arithmetic and copies ran while one was open for 3% of the time, Pallas kernels for 0%

commit v1 on v0

v1 whole, which is shorter than its diff:
```python
import functools
import math

import jax
import jax.numpy as jnp
import ml_dtypes
import numpy as np
from jax import lax
from jax.experimental import pallas as pl
from jax.experimental.pallas import tpu as pltpu
from jax.sharding import PartitionSpec as P

F = 640
LAGS = 512
VS = 4
SLOTS = 8
WINDOWS = 128
NG = F // 8
ZS = 8
YS = 4
STAGES = ((0,), (1,), (2, 3))
MESH = pl.DeviceIdType.MESH
OFFSETS = ((1, 0), (0, 1), (1, 2), (0, 3), (1, 1), (0, 2), (1, 3))


def lag_rows():
    bins = np.arange(F)
    shifts = np.arange(LAGS) - LAGS // 2
    angles = math.pi / F * (shifts[:, None] * bins[None, :] % (2 * F))
    factor = 1.0 / math.sqrt(2.0 * WINDOWS * F)
    cos = (np.cos(angles) * factor).reshape(LAGS, NG, 1, 8)
    sin = (-np.sin(angles) * factor).reshape(LAGS, NG, 1, 8)
    return np.concatenate([cos, sin], axis=2).reshape(LAGS, 2 * F).astype(ml_dtypes.bfloat16)


def group_receivers(spec, rb, first, count):
    def step(n, carry):
        q = first + n
        x = spec[:, :, pl.ds(pl.multiple_of(q * 16, 16), 16), :].astype(jnp.float32)
        rb[2 * q] = x[:, :, :8, :].reshape(256, 128).astype(jnp.bfloat16)
        rb[2 * q + 1] = x[:, :, 8:, :].reshape(256, 128).astype(jnp.bfloat16)
        return carry

    lax.fori_loop(0, count, step, 0, unroll=2)


def own_sources(spec, turned, store):
    lane = lax.broadcasted_iota(jnp.int32, (256, 128), 1)
    for part in range(3):
        count = 32 if part < 2 else 16

        def step(q, acc, part=part):
            at = pl.multiple_of(part * 256 + q * 16, 16)
            x = spec[:, :, pl.ds(at, 16), :].astype(jnp.float32)
            low = jnp.where(lane < VS, x[:, :, :8, :].reshape(256, 128), 0.0)
            high = jnp.where(lane < VS, x[:, :, 8:, :].reshape(256, 128), 0.0)
            return acc + pltpu.roll(low, q * 8, 1) + pltpu.roll(high, q * 8 + 4, 1)

        acc = lax.fori_loop(0, count // 2, step, jnp.zeros((256, 128), jnp.float32), unroll=2)
        rows = acc.T
        for p in range(2):
            turned[p, part * 128 : part * 128 + count * VS, :] = rows[: count * VS, p * 128 : (p + 1) * 128]
    for s in range(VS):
        for p in range(2):
            store(s, p, turned[p, pl.ds(s, NG, stride=VS), :].astype(jnp.bfloat16))


def cross(rb, wide, crossed, count, first, groups):
    row = lax.broadcasted_iota(jnp.int32, (8, 128), 0)
    lane = lax.broadcasted_iota(jnp.int32, (8, 128), 1)
    mask = (lane % 8 == row).astype(jnp.float32)

    def step(n, carry):
        g = first + n
        left, right = [], []
        for si in range(count):
            for k in range(SLOTS):
                re = wide[si, 0, k, pl.ds(g, 1), :] * mask
                im = wide[si, 1, k, pl.ds(g, 1), :] * mask
                left.append(jnp.concatenate([re, im], 0).astype(jnp.bfloat16))
                right.append(jnp.concatenate([im, -re], 0).astype(jnp.bfloat16))
        rows = jnp.concatenate([jnp.concatenate(left, 0), jnp.concatenate(right, 0)], 1)
        got = jnp.dot(rows, rb[g], preferred_element_type=jnp.float32).astype(jnp.bfloat16)
        at = pl.multiple_of(g * 16, 16)
        for si in range(count):
            part = got[si * 128 : (si + 1) * 128].reshape(SLOTS, 16, 128)
            crossed[:, pl.ds(at, 16), si * 128 : (si + 1) * 128] = part
        return carry

    lax.fori_loop(0, groups, step, 0, unroll=min(groups, 8))


class Gather:
    def __init__(self, stage, buf, recv, send, place):
        self.stage, self.buf, self.recv, self.send = stage, buf, recv, send
        self.xl, self.z, self.c, self.grp = place

    def block(self, x_flip, dz):
        x = 1 - self.xl if x_flip else self.xl
        return (self.c * 2 + x) * ZS + lax.rem(self.z + dz + ZS, ZS)

    def device(self, xl, z, c):
        return (xl * (2 * ZS) + z * 2 + c, self.grp)

    def copy(self, block, to, recv, send):
        ref = self.buf.at[block]
        xl, z, c = self.xl, self.z, self.c
        if to == "x":
            xl = 1 - xl
        elif to == "core":
            c = 1 - c
        elif to == "up":
            z = lax.rem(z + 1, ZS)
        elif to == "down":
            z = lax.rem(z + ZS - 1, ZS)
        return pltpu.make_async_remote_copy(
            src_ref=ref,
            dst_ref=ref,
            send_sem=self.send.at[self.stage, send],
            recv_sem=self.recv.at[self.stage, recv],
            device_id=self.device(xl, z, c),
            device_id_type=MESH,
        )

    def ring(self, x_flip, up, h):
        return {(0, 1): 0, (0, 0): 4, (1, 1): 7, (1, 0): 10}[(x_flip, up)] + h

    def reach(self, x_flip, up):
        return 4 if x_flip != up else 3

    def forward(self, x_flip, up, h):
        if h < self.reach(x_flip, up):
            block = self.block(x_flip, -h if up else h)
            self.copy(block, "up" if up else "down", self.ring(x_flip, up, h + 1), 2).start()

    def start(self):
        own = self.block(0, 0)
        self.copy(own, "x", 0, 0).start()
        self.forward(0, 1, 0)
        self.forward(0, 0, 0)
        self.copy(own, "core", 15, 1).start()

    def partner(self):
        block = self.block(1, 0)
        self.copy(block, "x", 0, 0).wait_recv()
        self.forward(1, 1, 0)
        self.forward(1, 0, 0)
        self.copy(block, "core", 15, 1).start()

    def hop(self, h):
        for x_flip in (0, 1):
            for up in (1, 0):
                if h <= self.reach(x_flip, up):
                    block = self.block(x_flip, -h if up else h)
                    self.copy(block, "x", self.ring(x_flip, up, h), 0).wait_recv()
                    self.forward(x_flip, up, h)
                    self.copy(block, "core", 15, 1).start()

    def finish(self):
        half = pl.ds((1 - self.c) * (2 * ZS), 2 * ZS)
        self.copy(half, "core", 15, 1).wait_recv()

    def steps(self):
        return [self.start, self.partner] + [functools.partial(self.hop, h) for h in (1, 2, 3, 4)] + [self.finish]

    def drain(self):
        self.copy(self.block(0, 0), "x", 0, 0).wait_send()
        self.copy(pl.ds(0, 2 * ZS), "core", 15, 1).wait_send()
        self.copy(pl.ds(0, 14), "up", 1, 2).wait_send()


def kernel(spec, table, pattern, slots, out, rb, turned, wide, crossed, parts, arrived, g_recv, g_send, r_recv, r_send, *bufs):
    blk, grp = lax.axis_index("blk"), lax.axis_index("grp")
    xl, z, c = blk // (2 * ZS), lax.rem(blk // 2, ZS), lax.rem(blk, 2)
    xh, y = grp // YS, lax.rem(grp, YS)
    gathers = [Gather(n, bufs[n], g_recv, g_send, (xl, z, c, grp)) for n in range(len(STAGES))]

    def peer(flip, dy):
        side = 1 - xh if flip else xh
        return side * YS + lax.rem(y + dy + YS, YS)

    barrier = pltpu.get_barrier_semaphore()
    near = [
        gathers[0].device(1 - xl, z, c),
        gathers[0].device(xl, z, 1 - c),
        gathers[0].device(xl, lax.rem(z + 1, ZS), c),
        gathers[0].device(xl, lax.rem(z + ZS - 1, ZS), c),
    ] + [(blk, peer(*offset)) for offset in OFFSETS]
    for device in near:
        pl.semaphore_signal(barrier, inc=1, device_id=device, device_id_type=MESH)

    own = gathers[0].block(0, 0)

    def store(s, p, rows):
        for n, stage in enumerate(STAGES):
            if s in stage:
                bufs[n][own, stage.index(s), :, p * 128 : (p + 1) * 128] = rows

    own_sources(spec, turned, store)
    pl.semaphore_wait(barrier, len(near))

    pump = iter([step for gather in gathers for step in gather.steps()])
    done = [0]

    def pump_to(count):
        while done[0] < count:
            next(pump)()
            done[0] += 1

    per = len(gathers[0].steps())
    pump_to(1)

    def look(i, found):
        on = pattern[i, blk] > 0
        at = (lax.rem(i, 2) * 2 + i // (2 * ZS)) * ZS + lax.rem(i // 2, ZS)
        slot = slots[i, blk]
        return tuple(jnp.where(on & (slot == k), at, found[k]) for k in range(SLOTS))

    found = lax.fori_loop(0, 4 * ZS, look, (jnp.int32(-1),) * SLOTS)
    for n in range(5):
        group_receivers(spec, rb, n * 8, 8)
        pump_to(2 + n)
    pump_to(per)

    for n, stage in enumerate(STAGES):
        count = len(stage)
        last = n + 1 == len(STAGES)
        begin = per * (n + 1)

        def reach(part, last=last, begin=begin):
            if not last:
                pump_to(begin + part)

        reach(1)
        for si in range(count):
            for k in range(SLOTS):
                present = jnp.where(found[k] >= 0, 1.0, 0.0)
                rows = bufs[n][jnp.maximum(found[k], 0), si].astype(jnp.float32) * present
                for p in range(2):
                    wide[si, p, k] = rows[:, p * 128 : (p + 1) * 128]
        for piece in range(5):
            cross(rb, wide, crossed, count, piece * 16, 16)
            if piece % 2 == 1:
                reach(2 + piece // 2)
        lanes = 128 * count
        for m, offset in enumerate(OFFSETS + ((0, 0),)):
            k = peer(*offset)
            got = jnp.dot(table[...], crossed[k, :, :lanes], preferred_element_type=jnp.float32)
            got = got.astype(jnp.bfloat16)
            target = parts if m < len(OFFSETS) else arrived
            for si, s in enumerate(stage):
                target[k, s] = got[:, si * 128 : (si + 1) * 128]
            if m < len(OFFSETS):
                send_part(parts, arrived, r_send, r_recv, n, m, k, grp, (blk, k)).start()
            if m in (1, 3, 5):
                reach(4 + m // 2)
        reach(per)

    for n, stage in enumerate(STAGES):
        for m, (flip, dy) in enumerate(OFFSETS):
            source = peer(flip, -dy)
            send_part(parts, arrived, r_send, r_recv, n, m, source, source, (blk, source)).wait_recv()
        for s in stage:
            total = arrived[0, s].astype(jnp.float32)
            for g in range(1, SLOTS):
                total += arrived[g, s].astype(jnp.float32)
            out[s] = total.astype(jnp.bfloat16)
    for n in range(len(STAGES)):
        gathers[n].drain()
        for m, offset in enumerate(OFFSETS):
            k = peer(*offset)
            send_part(parts, arrived, r_send, r_recv, n, m, k, grp, (blk, k)).wait_send()


def send_part(parts, arrived, send, recv, n, m, k, row, device):
    stage = pl.ds(STAGES[n][0], len(STAGES[n]))
    return pltpu.make_async_remote_copy(
        src_ref=parts.at[k, stage],
        dst_ref=arrived.at[row, stage],
        send_sem=send.at[n, m],
        recv_sem=recv.at[n, m],
        device_id=device,
        device_id_type=MESH,
    )


def per_device(spectra, pattern, slot_of_pair, table):
    most = max(len(stage) for stage in STAGES)
    vmem = pl.BlockSpec(memory_space=pltpu.VMEM)
    smem = pl.BlockSpec(memory_space=pltpu.SMEM)
    stacks = pl.pallas_call(
        kernel,
        out_shape=jax.ShapeDtypeStruct((VS, LAGS, 128), jnp.bfloat16),
        in_specs=[vmem, vmem, smem, smem],
        out_specs=vmem,
        scratch_shapes=[
            pltpu.VMEM((NG, 256, 128), jnp.bfloat16),
            pltpu.VMEM((2, 3 * 128, 128), jnp.float32),
            pltpu.VMEM((most, 2, SLOTS, NG, 128), jnp.float32),
            pltpu.VMEM((SLOTS, 2 * F, 128 * most), jnp.bfloat16),
            pltpu.VMEM((SLOTS, VS, LAGS, 128), jnp.bfloat16),
            pltpu.VMEM((SLOTS, VS, LAGS, 128), jnp.bfloat16),
            pltpu.SemaphoreType.DMA((len(STAGES), 16)),
            pltpu.SemaphoreType.DMA((len(STAGES), 3)),
            pltpu.SemaphoreType.DMA((len(STAGES), len(OFFSETS))),
            pltpu.SemaphoreType.DMA((len(STAGES), len(OFFSETS))),
        ]
        + [pltpu.VMEM((4 * ZS, len(stage), NG, 256), jnp.bfloat16) for stage in STAGES],
        compiler_params=pltpu.CompilerParams(collective_id=0, has_side_effects=True, vmem_limit_bytes=56 << 20),
        name="correlate",
    )(spectra, table, pattern, slot_of_pair)
    return jnp.transpose(stacks, (1, 0, 2))[None]


def solution(mesh):
    mapped = jax.shard_map(
        per_device,
        mesh=mesh,
        in_specs=(P(None, "grp", None, "blk"), P(), P(), P()),
        out_specs=P("grp", None, None, "blk"),
        check_vma=False,
    )
    return lambda spectra, pattern, slot_of_pair: mapped(spectra, pattern, slot_of_pair, jnp.asarray(lag_rows()))
```

time: 442 us -> 106 us (0.24)
  waiting for transfers between devices: 270 us -> 0 us
  Pallas kernels: 0 us -> 103 us
  local copies, waits for them, and re-layouts: 84.7 us -> 2.24 us
  matrix products: 29.6 us -> 0 us
  loops' own time: 27.7 us -> 0 us
  between operations: 13.4 us -> 0.01 us
  other arithmetic: 12.6 us -> 0 us
    reduce_scatter x1 -> x0, waiting for transfers between devices: 212 us -> none  [per_device(): summed = lax.psum_scatter(buffer, 'grp', scatter_dimension=0, tiled=True)]
    pallas_call x0 -> x1, Pallas kernels: none -> 103 us  [per_device(): pl.pallas_call(kernel, out_shape=jax.ShapeDtypeStruct((VS, LAGS, 128), jn...]
    all_gather x1 -> x0, waiting for transfers between devices: 58.8 us -> none  [per_device(): lax.all_gather(own_sources, 'blk', axis=0, tiled=True)]
    dynamic_slice x41 -> x0, local copies, waits for them, and re-layouts: 50.7 us -> none  [the longest x32 40.8 us: add_pair(): active = pattern[source_block, column] > 0]
    dot_general x9 -> x0, matrix products: 29.6 us -> none  [the longest x3 13.5 us: cross_spectra(): jnp.einsum('pgwsf,pgwfc->gfsc', sources, receivers, preferred_element_typ...]
    another operation x33 -> x0, loops' own time: 27.7 us -> none  [the longest x1 21.6 us: visit_all(): return lax.fori_loop(0, portion.shape[0], visit, buffer)]
    unnamed x2 -> x0, local copies, waits for them, and re-layouts: 13 us -> none
    while x1 -> x0, local copies, waits for them, and re-layouts: 9.12 us -> none  [visit_all(): return lax.fori_loop(0, portion.shape[0], visit, buffer)]
  transfers between devices with their start and end apart: 2 -> 0, of which waited for: 2 -> 0; matrix products, arithmetic and copies ran while one was open for 3% -> 0% of each run, Pallas kernels for 0% -> 0%
where the time goes in v1:
time: 106 us; the launch traced here: 105 us
  Pallas kernels  103 us (97%)
  local copies, waits for them, and re-layouts  2.24 us (2%)
    pallas_call x1, Pallas kernels, per_device(): pl.pallas_call(kernel, out_shape=jax.ShapeDtypeStruct((VS, LAGS, 128), jn...  103 us
    broadcast_in_dim x1, local copies, waits for them, and re-layouts, per_device(): return jnp.transpose(stacks, (1, 0, 2))[None]  2.24 us

profile of v1, /device:TPU:1, one launch (start us, length us, event | category | flops | bytes accessed | tf_op | source)
XLA Modules:
  0.0 105.0 jit_solution(16361760641112006643)
XLA Ops:
  0.0 102.8 %correlate.1 = bf16[4,512,128]{2,1,0:T(8,128)(2,1)} custom-call(bf16[2,16,640,128]{3,2,1,0:T(8,128)(2,1)} %spec.1, bf16[512,1280]{1,0:T(8,128)(2,1)} %constant.2.clone.table, s32[32,32]{1,0:T(8,128)} %pattern.1, s32[32,32]{1,0:T(8,128)} %slots.1), custom_call_target="tpu_custom_call" | custom-call | tf_op jit(solution)/shard_map/correlate/pallas_call | solution.py:291
  102.8 2.2 %copy.5 = bf16[1,512,4,128]{3,2,1,0:T(4,128)(2,1)} copy(bf16[1,512,4,128]{3,1,2,0:T(8,128)(2,1)} %bitcast.3) | data formatting | bytes 1048576 | tf_op jit(solution)/shard_map/broadcast_in_dim | solution.py:312

commit v2 on v0

v2 whole, which is shorter than its diff:
```python
import functools
import math

import jax
import jax.numpy as jnp
import ml_dtypes
import numpy as np
from jax import lax
from jax.experimental import pallas as pl
from jax.experimental.pallas import tpu as pltpu
from jax.sharding import PartitionSpec as P

F = 640
LAGS = 512
VS = 4
SLOTS = 8
WINDOWS = 128
NG = F // 8
ZS = 8
YS = 4
NQ = NG // 2
MESH = pl.DeviceIdType.MESH
FIRST = 256
REST = LAGS - FIRST


def lag_rows():
    bins = np.arange(F)
    shifts = np.arange(LAGS) - LAGS // 2
    angles = math.pi / F * (shifts[:, None] * bins[None, :] % (2 * F))
    factor = 1.0 / math.sqrt(2.0 * WINDOWS * F)
    both = np.stack([np.cos(angles), -np.sin(angles)], axis=1) * factor
    both = both.reshape(LAGS, 2, NQ, 2, 8).transpose(0, 3, 2, 1, 4)
    return both.reshape(LAGS, 2 * F).astype(ml_dtypes.bfloat16)


def group_receivers(spec, rb, first, count):
    def step(n, carry):
        q = first + n
        x = spec[:, :, pl.ds(pl.multiple_of(q * 16, 16), 16), :].astype(jnp.float32)
        rb[q] = x[:, :, :8, :].reshape(256, 128).astype(jnp.bfloat16)
        rb[NQ + q] = x[:, :, 8:, :].reshape(256, 128).astype(jnp.bfloat16)
        return carry

    lax.fori_loop(0, count, step, 0, unroll=2)


def own_sources(spec, turned, loaded, store):
    lane = lax.broadcasted_iota(jnp.int32, (8, 128), 1)
    for begin, count in ((0, 32), (32, NQ - 32)):

        def step(q, acc, begin=begin):
            x = spec[:, :, pl.ds(pl.multiple_of((begin + q) * 16, 16), 16), :].astype(jnp.float32)
            x = jnp.where(lane < VS, x.reshape(32, 2, 8, 128), 0.0).reshape(512, 128)
            return acc + pltpu.roll(x, q * VS, 1)

        acc = jnp.zeros((512, 128), jnp.float32)
        for chunk in range(count // 8):
            loaded(begin // 8 + chunk)
            acc = lax.fori_loop(chunk * 8, chunk * 8 + 8, step, acc, unroll=8)
        acc = acc.reshape(32, 2, 8, 128)
        for h in range(2):
            rows = acc[:, h].reshape(256, 128).T
            for p in range(2):
                turned[h, p, begin * VS : (begin + count) * VS, :] = rows[: count * VS, p * 128 : (p + 1) * 128]
    for s in range(VS):
        for h in range(2):
            for p in range(2):
                store(s, h, p, turned[h, p, pl.ds(s, NQ, stride=VS), :].astype(jnp.bfloat16))


def cross(rb, wide, crossed, count, first, groups):
    row = lax.broadcasted_iota(jnp.int32, (8, 128), 0)
    lane = lax.broadcasted_iota(jnp.int32, (8, 128), 1)
    mask = (lane % 8 == row).astype(jnp.float32)

    def step(n, carry):
        g = first + n
        left, right = [], []
        for si in range(count):
            for k in range(SLOTS):
                re = wide[si, 0, k, pl.ds(g, 1), :] * mask
                im = wide[si, 1, k, pl.ds(g, 1), :] * mask
                left.append(jnp.concatenate([re, im], 0).astype(jnp.bfloat16))
                right.append(jnp.concatenate([im, -re], 0).astype(jnp.bfloat16))
        rows = jnp.concatenate([jnp.concatenate(left, 0), jnp.concatenate(right, 0)], 1)
        got = jnp.dot(rows, rb[g], preferred_element_type=jnp.float32).astype(jnp.bfloat16)
        at = pl.multiple_of(g * 16, 16)
        for si in range(count):
            part = got[si * 128 : (si + 1) * 128].reshape(SLOTS, 16, 128)
            crossed[:, pl.ds(at, 16), si * 128 : (si + 1) * 128] = part
        return carry

    lax.fori_loop(0, groups, step, 0, unroll=16)


class Place:
    def __init__(self):
        blk, grp = lax.axis_index("blk"), lax.axis_index("grp")
        self.blk, self.grp = blk, grp
        self.xl, self.z, self.c = blk // (2 * ZS), lax.rem(blk // 2, ZS), lax.rem(blk, 2)
        self.xh, self.y = grp // YS, lax.rem(grp, YS)

    def near(self, flip_x=False, dz=0, flip_core=False):
        xl = 1 - self.xl if flip_x else self.xl
        c = 1 - self.c if flip_core else self.c
        return (xl * (2 * ZS) + lax.rem(self.z + dz + ZS, ZS) * 2 + c, self.grp)

    def far(self, flip_x=False, dy=0):
        xh = 1 - self.xh if flip_x else self.xh
        return (self.blk, xh * YS + lax.rem(self.y + dy, YS))


OWN = 2
X_SEND, CORE_SEND, Z_SEND = 0, 1, 2
CORE_RECV = 15


def at_z(dz):
    return (dz + OWN) % ZS


class Gather:
    def __init__(self, n, buf, recv, send, place):
        self.buf, self.recv, self.send, self.place = buf, recv.at[n], send.at[n], place

    def copy(self, src, dst, to, recv, send):
        return pltpu.make_async_remote_copy(
            src_ref=self.buf.at[pl.ds(*src)],
            dst_ref=self.buf.at[pl.ds(*dst)],
            send_sem=self.send.at[send],
            recv_sem=self.recv.at[recv],
            device_id=to,
            device_id_type=MESH,
        )

    def wait(self, blocks, recv):
        self.copy(blocks, blocks, self.place.near(True), recv, X_SEND).wait_recv()

    def to_core(self, first, count):
        self.copy((first, count), (2 * ZS + first, count), self.place.near(flip_core=True), CORE_RECV, CORE_SEND).start()

    def finish(self):
        self.wait((2 * ZS, 2 * ZS), CORE_RECV)

    def drain(self):
        for count, send in ((self.X_BLOCKS, X_SEND), (2 * ZS, CORE_SEND), (self.Z_BLOCKS, Z_SEND)):
            self.copy((0, count), (0, count), self.place.near(True), 0, send).wait_send()


class Ring(Gather):
    X_BLOCKS, Z_BLOCKS = 1, 14

    @staticmethod
    def index(flip_x, dz, flip_core):
        return (flip_core * ZS + lax.rem(dz + OWN, ZS)) * 2 + flip_x

    def start(self):
        self.copy((2 * OWN, 1), (2 * OWN + 1, 1), self.place.near(True), 0, X_SEND).start()

    def partner(self):
        self.wait((2 * OWN + 1, 1), 0)
        for sign, first in ((1, 1), (-1, 5)):
            self.copy((2 * OWN, 2), (2 * at_z(-sign), 2), self.place.near(dz=sign), first, Z_SEND).start()
        self.to_core(2 * OWN, 2)

    def hop(self, h):
        for sign, first in ((1, 0), (-1, 4)):
            single = 0 if sign > 0 else 1
            here, there = 2 * at_z(-h * sign), 2 * at_z(-(h + 1) * sign)
            blocks = (here, 2) if h < 4 else (here + single, 1)
            self.wait(blocks, first + h)
            ahead = self.place.near(dz=sign)
            if h < 3:
                self.copy(blocks, (there, 2), ahead, first + h + 1, Z_SEND).start()
            elif h == 3:
                self.copy((here + single, 1), (there + single, 1), ahead, first + 4, Z_SEND).start()
            self.to_core(*blocks)

    def steps(self):
        return [self.start, self.partner] + [functools.partial(self.hop, h) for h in (1, 2, 3, 4)] + [self.finish]


class Direct(Gather):
    X_BLOCKS, Z_BLOCKS = 8, 7
    NEAR, FAR = (0, 5), (5, 3)

    @staticmethod
    def index(flip_x, dz, flip_core):
        return (flip_core * 2 + flip_x) * ZS + lax.rem(dz + OWN, ZS)

    def start(self):
        for dz in (1, -1, 2, -2):
            self.copy((OWN, 1), (at_z(-dz), 1), self.place.near(dz=dz), 0, Z_SEND).start()

    def onward(self, blocks, recv):
        first, count = blocks
        self.copy(blocks, (ZS + first, count), self.place.near(True), recv, X_SEND).start()
        self.to_core(*blocks)

    def second(self):
        place = self.place
        self.wait((0, 4), 0)
        for sign in (1, -1):
            self.copy((at_z(-2 * sign), 1), (at_z(-3 * sign), 1), place.near(dz=sign), 1, Z_SEND).start()
        sign = 1 - 2 * place.c
        self.copy((OWN - 2 * sign, 1), (at_z(4), 1), place.near(dz=2 * sign), 1, Z_SEND).start()
        self.onward(self.NEAR, 2)

    def third(self):
        self.wait(self.FAR, 1)
        self.onward(self.FAR, 3)

    def from_x(self, blocks, recv):
        first, count = blocks
        self.wait((ZS + first, count), recv)
        self.to_core(ZS + first, count)

    def steps(self):
        return [
            self.start,
            self.second,
            self.third,
            lambda: self.from_x(self.NEAR, 2),
            lambda: self.from_x(self.FAR, 3),
            self.finish,
        ]


class Reduce:
    def __init__(self, s, place, bufs, send, recv):
        self.s, self.place = s, place
        self.parts, self.over_x, self.after_x, self.over_y, self.side, self.after_y = (buf.at[s] for buf in bufs)
        self.send, self.recv = send.at[s], recv.at[s]

    def copy(self, src, dst, sem, to):
        return pltpu.make_async_remote_copy(
            src_ref=src,
            dst_ref=dst,
            send_sem=self.send.at[sem],
            recv_sem=self.recv.at[sem],
            device_id=to,
            device_id_type=MESH,
        )

    def sent_slot(self, dy):
        place = self.place
        at = lax.rem(place.y + dy, YS)
        src = self.parts.at[1 - place.xh, at, pl.ds(0, FIRST)]
        self.copy(src, self.over_x.at[at], 0, place.far(True)).start()

    def sent_row(self, dy):
        at = lax.rem(self.place.y + dy, YS)
        src = self.parts.at[:, at, pl.ds(FIRST, REST)]
        self.copy(src, self.over_y.at[dy - 1], 1, self.place.far(dy=dy)).start()

    def wait(self, ref, sem):
        self.copy(ref, ref, sem, self.place.far(True)).wait_recv()

    def combine_x(self):
        place = self.place
        self.wait(self.over_x, 0)
        for dy in (2, 1, 3):
            at = lax.rem(place.y + dy, YS)
            own = self.parts[place.xh, at, :FIRST].astype(jnp.float32)
            self.over_x[at] = (own + self.over_x[at].astype(jnp.float32)).astype(jnp.bfloat16)
            self.copy(self.over_x.at[at], self.after_x.at[dy - 1], 2, place.far(dy=dy)).start()

    def along_y(self, xh):
        total = self.parts[xh, self.place.y, FIRST:].astype(jnp.float32)
        for m in range(YS - 1):
            total += self.over_y[m, xh].astype(jnp.float32)
        return total

    def combine_y(self):
        self.wait(self.over_y, 1)
        self.side[...] = self.along_y(1 - self.place.xh).astype(jnp.bfloat16)
        self.copy(self.side, self.after_y, 3, self.place.far(True)).start()

    def final(self, out):
        place, s = self.place, self.s
        self.wait(self.after_x, 2)
        total = self.parts[place.xh, place.y, :FIRST].astype(jnp.float32)
        total += self.over_x[place.y].astype(jnp.float32)
        for m in range(YS - 1):
            total += self.after_x[m].astype(jnp.float32)
        out[pl.ds(s, FIRST, stride=VS), :] = total
        rest = self.along_y(place.xh)
        self.wait(self.after_y, 3)
        out[pl.ds(FIRST * VS + s, REST, stride=VS), :] = rest + self.after_y[...].astype(jnp.float32)

    def drain(self):
        for ref, sem in ((self.over_x, 0), (self.over_y, 1), (self.after_x, 2), (self.after_y, 3)):
            self.copy(ref, ref, sem, self.place.far(True)).wait_send()


STAGES = ((0,), (1,), (2, 3))
KINDS = (Direct, Ring, Ring)
MOST = max(len(stage) for stage in STAGES)
PROGRAM = (
    ("gather", 0),
    ("gather", 1),
    ("gather", 2),
    ("group", 0),
    ("group", 1),
    ("group", 2),
    ("group", 3),
    ("group", 4),
    ("gather", 1),
    ("gather", 2),
    ("gather", 0),
    ("gather", 1),
    ("gather", 0),
    ("gather", 0),
    ("gather", 2),
    ("gather", 1),
    ("gather", 0),
    ("gather", 0),
    ("select", 0),
    ("cross", 0, 0),
    ("cross", 0, 1),
    ("cross", 0, 2),
    ("cross", 0, 3),
    ("cross", 0, 4),
    ("lags", 0, 0),
    ("gather", 1),
    ("gather", 2),
    ("lags", 0, 1),
    ("lags", 0, 2),
    ("lags", 0, 3),
    ("gather", 1),
    ("gather", 1),
    ("select", 1),
    ("cross", 1, 0),
    ("cross", 1, 1),
    ("cross", 1, 2),
    ("gather", 2),
    ("cross", 1, 3),
    ("after_y", 0),
    ("cross", 1, 4),
    ("lags", 1, 0),
    ("after_x", 0),
    ("lags", 1, 1),
    ("gather", 2),
    ("lags", 1, 2),
    ("lags", 1, 3),
    ("gather", 2),
    ("select", 2),
    ("cross", 2, 0),
    ("cross", 2, 1),
    ("cross", 2, 2),
    ("cross", 2, 3),
    ("cross", 2, 4),
    ("lags", 2, 0),
    ("after_x", 1),
    ("lags", 2, 1),
    ("after_y", 1),
    ("lags", 2, 2),
    ("lags", 2, 3),
    ("final", 0),
    ("final", 1),
    ("after_x", 2),
    ("after_x", 3),
    ("after_y", 2),
    ("after_y", 3),
    ("final", 2),
    ("final", 3),
)


def kernel(spectra, lag_table, pattern, slots, out, rb, turned, wide, crossed, spec, table, load, *rest):
    sums, (g_send, g_recv, r_send, r_recv), bufs = rest[:6], rest[6:10], rest[10:]
    loads = []
    for n in range(5):
        bins = pl.ds(n * 128, 128)
        loads.append(pltpu.make_async_copy(spectra.at[:, :, bins], spec.at[:, :, bins], load.at[n]))
    loads.append(pltpu.make_async_copy(lag_table, table, load.at[5]))
    for copy in loads:
        copy.start()
    place = Place()
    blk = place.blk
    barrier = pltpu.get_barrier_semaphore()
    peers = [place.near(True), place.near(flip_core=True)] + [place.near(dz=dz) for dz in (1, -1, 2, -2)]
    peers += [place.far(True)] + [place.far(dy=dy) for dy in (1, 2, 3)]
    for device in peers:
        pl.semaphore_signal(barrier, inc=1, device_id=device, device_id_type=MESH)

    def store(s, h, p, rows):
        for n, stage in enumerate(STAGES):
            if s in stage:
                own = 2 * OWN if KINDS[n] is Ring else OWN
                bufs[n][own, stage.index(s), h * NQ : (h + 1) * NQ, p * 128 : (p + 1) * 128] = rows

    own_sources(spec, turned, lambda n: loads[n].wait(), store)
    pl.semaphore_wait(barrier, len(peers))

    gathers = [KINDS[n](n, bufs[n], g_recv, g_send, place) for n in range(len(STAGES))]
    reduces = [Reduce(s, place, sums, r_send, r_recv) for s in range(VS)]
    steps = [iter(gather.steps()) for gather in gathers]

    def look(i, found):
        on = pattern[i, blk] > 0
        flip_x = jnp.abs(i // (2 * ZS) - place.xl)
        flip_core = jnp.abs(lax.rem(i, 2) - place.c)
        dz = lax.rem(lax.rem(i // 2, ZS) - place.z + ZS, ZS)
        slot = slots[i, blk]
        rule = [kind.index(flip_x, dz, flip_core) for kind in (Direct, Ring)]
        return tuple(
            tuple(jnp.where(on & (slot == k), at, old[k]) for k in range(SLOTS)) for at, old in zip(rule, found)
        )

    found = lax.fori_loop(0, 4 * ZS, look, ((jnp.int32(-1),) * SLOTS,) * 2)

    loads[5].wait()

    def select(n):
        block = found[0 if KINDS[n] is Direct else 1]
        for k in range(SLOTS):
            present = jnp.where(block[k] >= 0, 1.0, 0.0)
            for si in range(len(STAGES[n])):
                rows = bufs[n][jnp.maximum(block[k], 0), si].astype(jnp.float32) * present
                for p in range(2):
                    wide[si, p, k] = rows[:, p * 128 : (p + 1) * 128]

    def lags(n, number):
        stage, dy = STAGES[n], (2, 1, 3, 0)[number]
        at = lax.rem(place.y + dy, YS)
        for other in (True, False):
            xh = 1 - place.xh if other else place.xh
            rows = crossed[xh * YS + at, :, : 128 * len(stage)]
            got = jnp.dot(table[...], rows, preferred_element_type=jnp.float32).astype(jnp.bfloat16)
            for si, s in enumerate(stage):
                sums[0][s, xh, at] = got[:, si * 128 : (si + 1) * 128]
                if other:
                    reduces[s].sent_slot(dy)
        if dy:
            for s in stage:
                reduces[s].sent_row(dy)

    run = {
        "gather": lambda n: next(steps[n])(),
        "group": lambda n: group_receivers(spec, rb, n * 8, 8),
        "select": select,
        "cross": lambda n, piece: cross(rb, wide, crossed, len(STAGES[n]), piece * 16, 16),
        "lags": lags,
        "after_x": lambda s: reduces[s].combine_x(),
        "after_y": lambda s: reduces[s].combine_y(),
        "final": lambda s: reduces[s].final(out),
    }
    for name, *arguments in PROGRAM:
        run[name](*arguments)
    for gather in gathers:
        gather.drain()
    for s in range(VS):
        reduces[s].drain()


def per_device(spectra, pattern, slot_of_pair, table):
    vmem = pl.BlockSpec(memory_space=pltpu.VMEM)
    smem = pl.BlockSpec(memory_space=pltpu.SMEM)
    hbm = pl.BlockSpec(memory_space=pl.ANY)
    stacks = pl.pallas_call(
        kernel,
        out_shape=jax.ShapeDtypeStruct((LAGS * VS, 128), jnp.float32),
        in_specs=[hbm, hbm, smem, smem],
        out_specs=vmem,
        scratch_shapes=[
            pltpu.VMEM((NG, 256, 128), jnp.bfloat16),
            pltpu.VMEM((2, 2, 2 * 128, 128), jnp.float32),
            pltpu.VMEM((MOST, 2, SLOTS, NG, 128), jnp.float32),
            pltpu.VMEM((SLOTS, 2 * F, 128 * MOST), jnp.bfloat16),
            pltpu.VMEM((2, WINDOWS // 8, F, 128), jnp.bfloat16),
            pltpu.VMEM((LAGS, 2 * F), jnp.bfloat16),
            pltpu.SemaphoreType.DMA((6,)),
            pltpu.VMEM((VS, 2, YS, LAGS, 128), jnp.bfloat16),
            pltpu.VMEM((VS, YS, FIRST, 128), jnp.bfloat16),
            pltpu.VMEM((VS, YS - 1, FIRST, 128), jnp.bfloat16),
            pltpu.VMEM((VS, YS - 1, 2, REST, 128), jnp.bfloat16),
            pltpu.VMEM((VS, REST, 128), jnp.bfloat16),
            pltpu.VMEM((VS, REST, 128), jnp.bfloat16),
            pltpu.SemaphoreType.DMA((len(STAGES), 3)),
            pltpu.SemaphoreType.DMA((len(STAGES), 16)),
            pltpu.SemaphoreType.DMA((VS, 4)),
            pltpu.SemaphoreType.DMA((VS, 4)),
                ]
        + [pltpu.VMEM((4 * ZS, len(stage), NG, 256), jnp.bfloat16) for stage in STAGES],
        compiler_params=pltpu.CompilerParams(collective_id=0, has_side_effects=True, vmem_limit_bytes=56 << 20),
        name="correlate",
    )(spectra, table, pattern, slot_of_pair)
    return stacks.astype(jnp.bfloat16).reshape(1, LAGS, VS, 128)


def solution(mesh):
    mapped = jax.shard_map(
        per_device,
        mesh=mesh,
        in_specs=(P(None, "grp", None, "blk"), P(), P(), P()),
        out_specs=P("grp", None, None, "blk"),
        check_vma=False,
    )
    return lambda spectra, pattern, slot_of_pair: mapped(spectra, pattern, slot_of_pair, jnp.asarray(lag_rows()))
```

time: 442 us -> 79.3 us (0.18)
  waiting for transfers between devices: 270 us -> 0 us
  local copies, waits for them, and re-layouts: 84.7 us -> 0 us
  Pallas kernels: 0 us -> 77 us
  matrix products: 29.6 us -> 0 us
  loops' own time: 27.7 us -> 0 us
  between operations: 13.4 us -> 0.01 us
  other arithmetic: 12.6 us -> 2.07 us
    reduce_scatter x1 -> x0, waiting for transfers between devices: 212 us -> none  [per_device(): summed = lax.psum_scatter(buffer, 'grp', scatter_dimension=0, tiled=True)]
    pallas_call x0 -> x1, Pallas kernels: none -> 77 us  [per_device(): pl.pallas_call(kernel, out_shape=jax.ShapeDtypeStruct((LAGS * VS, 128), j...]
    all_gather x1 -> x0, waiting for transfers between devices: 58.8 us -> none  [per_device(): lax.all_gather(own_sources, 'blk', axis=0, tiled=True)]
    dynamic_slice x41 -> x0, local copies, waits for them, and re-layouts: 50.7 us -> none  [the longest x32 40.8 us: add_pair(): active = pattern[source_block, column] > 0]
    dot_general x9 -> x0, matrix products: 29.6 us -> none  [the longest x3 13.5 us: cross_spectra(): jnp.einsum('pgwsf,pgwfc->gfsc', sources, receivers, preferred_element_typ...]
    another operation x33 -> x0, loops' own time: 27.7 us -> none  [the longest x1 21.6 us: visit_all(): return lax.fori_loop(0, portion.shape[0], visit, buffer)]
    unnamed x2 -> x0, local copies, waits for them, and re-layouts: 13 us -> none
    while x1 -> x0, local copies, waits for them, and re-layouts: 9.12 us -> none  [visit_all(): return lax.fori_loop(0, portion.shape[0], visit, buffer)]
  transfers between devices with their start and end apart: 2 -> 0, of which waited for: 2 -> 0; matrix products, arithmetic and copies ran while one was open for 3% -> 0% of each run, Pallas kernels for 0% -> 0%
where the time goes in v2:
time: 79.3 us; the launch traced here: 79.1 us
  Pallas kernels  77 us (97%)
  other arithmetic  2.07 us (3%)
    pallas_call x1, Pallas kernels, per_device(): pl.pallas_call(kernel, out_shape=jax.ShapeDtypeStruct((LAGS * VS, 128), j...  77 us
    convert_element_type x1, other arithmetic, per_device(): return stacks.astype(jnp.bfloat16).reshape(1, LAGS, VS, 128)  2.07 us

profile of v2, /device:TPU:1, one launch (start us, length us, event | category | flops | bytes accessed | tf_op | source)
XLA Modules:
  0.0 79.1 jit_solution(16193945433709800859)
XLA Ops:
  0.0 77.0 %correlate.1 = f32[2048,128]{1,0:T(8,128)} custom-call(bf16[2,16,640,128]{3,2,1,0:T(8,128)(2,1)} %spectra.1, bf16[512,1280]{1,0:T(8,128)(2,1)} %constant.2.clone.lag_table, s32[32,32]{1,0:T(8,128)} %pattern.1, s32[32,32]{1,0:T(8,128)} %slots.1), custom_call_target="tpu_custom_call" | custom-call | tf_op jit(solution)/shard_map/correlate/pallas_call | solution.py:462
  77.0 2.1 %convert_element_type.3 = bf16[2048,128]{1,0:T(8,128)(2,1)} convert(f32[2048,128]{1,0:T(8,128)} %correlate.1) | non-fusion elementwise | flops 262144 | bytes 1572864 | tf_op jit(solution)/shard_map/convert_element_type | solution.py:490

commit v3 on v2

--- a/solution.py
+++ b/solution.py
@@ -22,6 +22,7 @@
 MESH = pl.DeviceIdType.MESH
 FIRST = 256
 REST = LAGS - FIRST
+HALF = REST // 2
 
 
 def lag_rows():
@@ -100,15 +101,27 @@
         self.blk, self.grp = blk, grp
         self.xl, self.z, self.c = blk // (2 * ZS), lax.rem(blk // 2, ZS), lax.rem(blk, 2)
         self.xh, self.y = grp // YS, lax.rem(grp, YS)
+        self.known = {}
+
+    def once(self, key, make):
+        if key not in self.known:
+            self.known[key] = make()
+        return self.known[key]
 
     def near(self, flip_x=False, dz=0, flip_core=False):
         xl = 1 - self.xl if flip_x else self.xl
         c = 1 - self.c if flip_core else self.c
-        return (xl * (2 * ZS) + lax.rem(self.z + dz + ZS, ZS) * 2 + c, self.grp)
+        at = lambda: xl * (2 * ZS) + lax.rem(self.z + dz + ZS, ZS) * 2 + c
+        if not isinstance(dz, int):
+            return (at(), self.grp)
+        return (self.once(("near", flip_x, dz, flip_core), at), self.grp)
+
+    def slot(self, flip_x, dy):
+        xh = 1 - self.xh if flip_x else self.xh
+        return self.once(("slot", flip_x, dy), lambda: xh * YS + lax.rem(self.y + dy, YS))
 
     def far(self, flip_x=False, dy=0):
-        xh = 1 - self.xh if flip_x else self.xh
-        return (self.blk, xh * YS + lax.rem(self.y + dy, YS))
+        return (self.blk, self.slot(flip_x, dy))
 
 
 OWN = 2
@@ -116,8 +129,8 @@
 CORE_RECV = 15
 
 
-def at_z(dz):
-    return (dz + OWN) % ZS
+def at_z(dz, own=OWN):
+    return (dz + own) % ZS
 
 
 class Gather:
@@ -149,25 +162,24 @@
 
 
 class Ring(Gather):
-    X_BLOCKS, Z_BLOCKS = 1, 14
+    X_BLOCKS, Z_BLOCKS, OWN = 1, 14, 1
 
     @staticmethod
     def index(flip_x, dz, flip_core):
-        return (flip_core * ZS + lax.rem(dz + OWN, ZS)) * 2 + flip_x
+        return (flip_core * ZS + lax.rem(dz + 1, ZS)) * 2 + flip_x
 
     def start(self):
-        self.copy((2 * OWN, 1), (2 * OWN + 1, 1), self.place.near(True), 0, X_SEND).start()
+        self.copy((2, 1), (3, 1), self.place.near(True), 0, X_SEND).start()
 
     def partner(self):
-        self.wait((2 * OWN + 1, 1), 0)
+        self.wait((3, 1), 0)
         for sign, first in ((1, 1), (-1, 5)):
-            self.copy((2 * OWN, 2), (2 * at_z(-sign), 2), self.place.near(dz=sign), first, Z_SEND).start()
-        self.to_core(2 * OWN, 2)
+            self.copy((2, 2), (2 * at_z(-sign, 1), 2), self.place.near(dz=sign), first, Z_SEND).start()
 
     def hop(self, h):
         for sign, first in ((1, 0), (-1, 4)):
             single = 0 if sign > 0 else 1
-            here, there = 2 * at_z(-h * sign), 2 * at_z(-(h + 1) * sign)
+            here, there = 2 * at_z(-h * sign, 1), 2 * at_z(-(h + 1) * sign, 1)
             blocks = (here, 2) if h < 4 else (here + single, 1)
             self.wait(blocks, first + h)
             ahead = self.place.near(dz=sign)
@@ -175,6 +187,7 @@
                 self.copy(blocks, (there, 2), ahead, first + h + 1, Z_SEND).start()
             elif h == 3:
                 self.copy((here + single, 1), (there + single, 1), ahead, first + 4, Z_SEND).start()
+        for blocks in {1: ((0, 6),), 3: ((6, 4), (12, 4)), 4: ((10, 2),)}.get(h, ()):
             self.to_core(*blocks)
 
     def steps(self):
@@ -227,11 +240,19 @@
         ]
 
 
+STAGES = ((0,), (1, 2), (3,))
+KINDS = (Direct, Ring, Ring)
+MOST = max(len(stage) for stage in STAGES)
+TURNS = (2, 1, 3, 0)
+
+
 class Reduce:
-    def __init__(self, s, place, bufs, send, recv):
-        self.s, self.place = s, place
-        self.parts, self.over_x, self.after_x, self.over_y, self.side, self.after_y = (buf.at[s] for buf in bufs)
-        self.send, self.recv = send.at[s], recv.at[s]
+    def __init__(self, n, place, bufs, send, recv):
+        self.stage, self.place = STAGES[n], place
+        part = pl.ds(STAGES[n][0], len(STAGES[n]))
+        refs = (buf.at[part] for buf in bufs)
+        self.parts, self.over_x, self.after_x, self.over_y, self.side, self.after_y, self.passing = refs
+        self.send, self.recv = send.at[n], recv.at[n]
 
     def copy(self, src, dst, sem, to):
         return pltpu.make_async_remote_copy(
@@ -243,60 +264,74 @@
             device_id_type=MESH,
         )
 
-    def sent_slot(self, dy):
-        place = self.place
-        at = lax.rem(place.y + dy, YS)
-        src = self.parts.at[1 - place.xh, at, pl.ds(0, FIRST)]
-        self.copy(src, self.over_x.at[at], 0, place.far(True)).start()
-
-    def sent_row(self, dy):
-        at = lax.rem(self.place.y + dy, YS)
-        src = self.parts.at[:, at, pl.ds(FIRST, REST)]
-        self.copy(src, self.over_y.at[dy - 1], 1, self.place.far(dy=dy)).start()
+    def sent(self, turn):
+        if turn % 2:
+            two = pl.ds(turn - 1, 2)
+            src = self.parts.at[:, 1, two, pl.ds(0, FIRST)]
+            self.copy(src, self.over_x.at[:, two], 0, self.place.far(True)).start()
+        if turn == 0:
+            for half, dy in ((0, 1), (1, 3)):
+                src = self.parts.at[:, :, 0, pl.ds(FIRST + half * HALF, HALF)]
+                self.copy(src, self.passing.at[:, :, half], 4, self.place.far(dy=dy)).start()
+        elif turn < YS - 1:
+            self.along(turn, turn % 2)
+
+    def along(self, turn, half):
+        rows = pl.ds(FIRST + half * HALF, HALF)
+        to = self.place.far(dy=TURNS[turn])
+        self.copy(self.parts.at[:, :, turn, rows], self.over_y.at[:, turn - 1, :, half], 1, to).start()
+
+    def relay(self):
+        self.wait(self.passing, 4)
+        for half in range(2):
+            begin = FIRST + half * HALF
+            for si in range(len(self.stage)):
+                for side in range(2):
+                    own = self.parts[si, side, 1 + half, begin : begin + HALF].astype(jnp.float32)
+                    own += self.passing[si, side, half].astype(jnp.float32)
+                    self.parts[si, side, 1 + half, begin : begin + HALF] = own.astype(jnp.bfloat16)
+            self.along(1 + half, half)
 
     def wait(self, ref, sem):
         self.copy(ref, ref, sem, self.place.far(True)).wait_recv()
 
     def combine_x(self):
-        place = self.place
         self.wait(self.over_x, 0)
-        for dy in (2, 1, 3):
-            at = lax.rem(place.y + dy, YS)
-            own = self.parts[place.xh, at, :FIRST].astype(jnp.float32)
-            self.over_x[at] = (own + self.over_x[at].astype(jnp.float32)).astype(jnp.bfloat16)
-            self.copy(self.over_x.at[at], self.after_x.at[dy - 1], 2, place.far(dy=dy)).start()
-
-    def along_y(self, xh):
-        total = self.parts[xh, self.place.y, FIRST:].astype(jnp.float32)
-        for m in range(YS - 1):
-            total += self.over_y[m, xh].astype(jnp.float32)
+        for turn in range(YS - 1):
+            for si in range(len(self.stage)):
+                own = self.parts[si, 0, turn, :FIRST].astype(jnp.float32)
+                self.over_x[si, turn] = (own + self.over_x[si, turn].astype(jnp.float32)).astype(jnp.bfloat16)
+            self.copy(self.over_x.at[:, turn], self.after_x.at[:, turn], 2, self.place.far(dy=TURNS[turn])).start()
+
+    def along_y(self, si, side):
+        total = self.parts[si, side, YS - 1, FIRST:].astype(jnp.float32)
+        for m in range(2):
+            total += self.over_y[si, m, side].astype(jnp.float32).reshape(REST, 128)
         return total
 
     def combine_y(self):
         self.wait(self.over_y, 1)
-        self.side[...] = self.along_y(1 - self.place.xh).astype(jnp.bfloat16)
+        for si in range(len(self.stage)):
+            self.side[si] = self.along_y(si, 1).astype(jnp.bfloat16)
         self.copy(self.side, self.after_y, 3, self.place.far(True)).start()
 
     def final(self, out):
-        place, s = self.place, self.s
         self.wait(self.after_x, 2)
-        total = self.parts[place.xh, place.y, :FIRST].astype(jnp.float32)
-        total += self.over_x[place.y].astype(jnp.float32)
-        for m in range(YS - 1):
-            total += self.after_x[m].astype(jnp.float32)
-        out[pl.ds(s, FIRST, stride=VS), :] = total
-        rest = self.along_y(place.xh)
         self.wait(self.after_y, 3)
-        out[pl.ds(FIRST * VS + s, REST, stride=VS), :] = rest + self.after_y[...].astype(jnp.float32)
+        for si, s in enumerate(self.stage):
+            total = self.parts[si, 0, YS - 1, :FIRST].astype(jnp.float32)
+            total += self.over_x[si, YS - 1].astype(jnp.float32)
+            for turn in range(YS - 1):
+                total += self.after_x[si, turn].astype(jnp.float32)
+            out[pl.ds(s, FIRST, stride=VS), :] = total
+            rest = self.along_y(si, 0) + self.after_y[si].astype(jnp.float32)
+            out[pl.ds(FIRST * VS + s, REST, stride=VS), :] = rest
 
     def drain(self):
-        for ref, sem in ((self.over_x, 0), (self.over_y, 1), (self.after_x, 2), (self.after_y, 3)):
+        for ref, sem in ((self.over_x, 0), (self.over_y, 1), (self.after_x, 2), (self.after_y, 3), (self.passing, 4)):
             self.copy(ref, ref, sem, self.place.far(True)).wait_send()
 
 
-STAGES = ((0,), (1,), (2, 3))
-KINDS = (Direct, Ring, Ring)
-MOST = max(len(stage) for stage in STAGES)
 PROGRAM = (
     ("gather", 0),
     ("gather", 1),
@@ -306,45 +341,46 @@
     ("group", 2),
     ("group", 3),
     ("group", 4),
-    ("gather", 1),
-    ("gather", 2),
     ("gather", 0),
     ("gather", 1),
     ("gather", 0),
+    ("gather", 2),
     ("gather", 0),
-    ("gather", 2),
     ("gather", 1),
     ("gather", 0),
+    ("gather", 2),
     ("gather", 0),
     ("select", 0),
     ("cross", 0, 0),
     ("cross", 0, 1),
     ("cross", 0, 2),
     ("cross", 0, 3),
+    ("gather", 1),
     ("cross", 0, 4),
     ("lags", 0, 0),
-    ("gather", 1),
-    ("gather", 2),
     ("lags", 0, 1),
+    ("gather", 2),
     ("lags", 0, 2),
     ("lags", 0, 3),
     ("gather", 1),
+    ("relay", 0),
+    ("gather", 2),
+    ("gather", 1),
+    ("after_x", 0),
+    ("gather", 2),
+    ("after_y", 0),
     ("gather", 1),
     ("select", 1),
     ("cross", 1, 0),
+    ("gather", 2),
     ("cross", 1, 1),
     ("cross", 1, 2),
-    ("gather", 2),
     ("cross", 1, 3),
-    ("after_y", 0),
     ("cross", 1, 4),
     ("lags", 1, 0),
-    ("after_x", 0),
     ("lags", 1, 1),
-    ("gather", 2),
     ("lags", 1, 2),
     ("lags", 1, 3),
-    ("gather", 2),
     ("select", 2),
     ("cross", 2, 0),
     ("cross", 2, 1),
@@ -352,24 +388,23 @@
     ("cross", 2, 3),
     ("cross", 2, 4),
     ("lags", 2, 0),
-    ("after_x", 1),
+    ("relay", 1),
     ("lags", 2, 1),
-    ("after_y", 1),
     ("lags", 2, 2),
     ("lags", 2, 3),
+    ("relay", 2),
     ("final", 0),
+    ("after_x", 1),
+    ("after_y", 1),
+    ("after_y", 2),
+    ("after_x", 2),
     ("final", 1),
-    ("after_x", 2),
-    ("after_x", 3),
-    ("after_y", 2),
-    ("after_y", 3),
     ("final", 2),
-    ("final", 3),
 )
 
 
 def kernel(spectra, lag_table, pattern, slots, out, rb, turned, wide, crossed, spec, table, load, *rest):
-    sums, (g_send, g_recv, r_send, r_recv), bufs = rest[:6], rest[6:10], rest[10:]
+    sums, (g_send, g_recv, r_send, r_recv), bufs = rest[:7], rest[7:11], rest[11:]
     loads = []
     for n in range(5):
         bins = pl.ds(n * 128, 128)
@@ -388,14 +423,14 @@
     def store(s, h, p, rows):
         for n, stage in enumerate(STAGES):
             if s in stage:
-                own = 2 * OWN if KINDS[n] is Ring else OWN
+                own = 2 if KINDS[n] is Ring else OWN
                 bufs[n][own, stage.index(s), h * NQ : (h + 1) * NQ, p * 128 : (p + 1) * 128] = rows
 
     own_sources(spec, turned, lambda n: loads[n].wait(), store)
     pl.semaphore_wait(barrier, len(peers))
 
     gathers = [KINDS[n](n, bufs[n], g_recv, g_send, place) for n in range(len(STAGES))]
-    reduces = [Reduce(s, place, sums, r_send, r_recv) for s in range(VS)]
+    reduces = [Reduce(n, place, sums, r_send, r_recv) for n in range(len(STAGES))]
     steps = [iter(gather.steps()) for gather in gathers]
 
     def look(i, found):
@@ -409,11 +444,16 @@
             tuple(jnp.where(on & (slot == k), at, old[k]) for k in range(SLOTS)) for at, old in zip(rule, found)
         )
 
-    found = lax.fori_loop(0, 4 * ZS, look, ((jnp.int32(-1),) * SLOTS,) * 2)
-
-    loads[5].wait()
+    found = []
+
+    def group(n):
+        if not found:
+            found.extend(lax.fori_loop(0, 4 * ZS, look, ((jnp.int32(-1),) * SLOTS,) * 2))
+        group_receivers(spec, rb, n * 8, 8)
 
     def select(n):
+        if n == 0:
+            loads[5].wait()
         block = found[0 if KINDS[n] is Direct else 1]
         for k in range(SLOTS):
             present = jnp.where(block[k] >= 0, 1.0, 0.0)
@@ -422,37 +462,31 @@
                 for p in range(2):
                     wide[si, p, k] = rows[:, p * 128 : (p + 1) * 128]
 
-    def lags(n, number):
-        stage, dy = STAGES[n], (2, 1, 3, 0)[number]
-        at = lax.rem(place.y + dy, YS)
-        for other in (True, False):
-            xh = 1 - place.xh if other else place.xh
-            rows = crossed[xh * YS + at, :, : 128 * len(stage)]
+    def lags(n, turn):
+        for side in (1, 0):
+            rows = crossed[place.slot(side == 1, TURNS[turn]), :, : 128 * len(STAGES[n])]
             got = jnp.dot(table[...], rows, preferred_element_type=jnp.float32).astype(jnp.bfloat16)
-            for si, s in enumerate(stage):
-                sums[0][s, xh, at] = got[:, si * 128 : (si + 1) * 128]
-                if other:
-                    reduces[s].sent_slot(dy)
-        if dy:
-            for s in stage:
-                reduces[s].sent_row(dy)
+            for si, s in enumerate(STAGES[n]):
+                sums[0][s, side, turn] = got[:, si * 128 : (si + 1) * 128]
+        reduces[n].sent(turn)
 
     run = {
         "gather": lambda n: next(steps[n])(),
-        "group": lambda n: group_receivers(spec, rb, n * 8, 8),
+        "group": group,
         "select": select,
         "cross": lambda n, piece: cross(rb, wide, crossed, len(STAGES[n]), piece * 16, 16),
         "lags": lags,
-        "after_x": lambda s: reduces[s].combine_x(),
-        "after_y": lambda s: reduces[s].combine_y(),
+        "relay": lambda n: reduces[n].relay(),
+        "after_x": lambda n: reduces[n].combine_x(),
+        "after_y": lambda n: reduces[n].combine_y(),
         "final": lambda s: reduces[s].final(out),
     }
     for name, *arguments in PROGRAM:
         run[name](*arguments)
     for gather in gathers:
         gather.drain()
-    for s in range(VS):
-        reduces[s].drain()
+    for reduce in reduces:
+        reduce.drain()
 
 
 def per_device(spectra, pattern, slot_of_pair, table):
@@ -475,13 +509,14 @@
             pltpu.VMEM((VS, 2, YS, LAGS, 128), jnp.bfloat16),
             pltpu.VMEM((VS, YS, FIRST, 128), jnp.bfloat16),
             pltpu.VMEM((VS, YS - 1, FIRST, 128), jnp.bfloat16),
-            pltpu.VMEM((VS, YS - 1, 2, REST, 128), jnp.bfloat16),
+            pltpu.VMEM((VS, 2, 2, 2, HALF, 128), jnp.bfloat16),
             pltpu.VMEM((VS, REST, 128), jnp.bfloat16),
             pltpu.VMEM((VS, REST, 128), jnp.bfloat16),
+            pltpu.VMEM((VS, 2, 2, HALF, 128), jnp.bfloat16),
             pltpu.SemaphoreType.DMA((len(STAGES), 3)),
             pltpu.SemaphoreType.DMA((len(STAGES), 16)),
-            pltpu.SemaphoreType.DMA((VS, 4)),
-            pltpu.SemaphoreType.DMA((VS, 4)),
+            pltpu.SemaphoreType.DMA((len(STAGES), 5)),
+            pltpu.SemaphoreType.DMA((len(STAGES), 5)),
                 ]
         + [pltpu.VMEM((4 * ZS, len(stage), NG, 256), jnp.bfloat16) for stage in STAGES],
         compiler_params=pltpu.CompilerParams(collective_id=0, has_side_effects=True, vmem_limit_bytes=56 << 20),

time: 79.3 us -> 74.3 us (0.937)
  Pallas kernels: 77 us -> 71.9 us
    pallas_call x1, Pallas kernels: 77 us -> 71.9 us  [per_device(): pl.pallas_call(kernel, out_shape=jax.ShapeDtypeStruct((LAGS * VS, 128), j...]
where the time goes in v3:
time: 74.3 us; the launch traced here: 74 us
  Pallas kernels  71.9 us (97%)
  other arithmetic  2.07 us (3%)
    pallas_call x1, Pallas kernels, per_device(): pl.pallas_call(kernel, out_shape=jax.ShapeDtypeStruct((LAGS * VS, 128), j...  71.9 us
    convert_element_type x1, other arithmetic, per_device(): return stacks.astype(jnp.bfloat16).reshape(1, LAGS, VS, 128)  2.07 us

profile of v3, /device:TPU:1, one launch (start us, length us, event | category | flops | bytes accessed | tf_op | source)
XLA Modules:
  0.0 74.0 jit_solution(10058356859150183041)
XLA Ops:
  0.0 71.9 %correlate.1 = f32[2048,128]{1,0:T(8,128)} custom-call(bf16[2,16,640,128]{3,2,1,0:T(8,128)(2,1)} %spectra.1, bf16[512,1280]{1,0:T(8,128)(2,1)} %constant.2.clone.lag_table, s32[32,32]{1,0:T(8,128)} %pattern.1, s32[32,32]{1,0:T(8,128)} %slots.1), custom_call_target="tpu_custom_call" | custom-call | tf_op jit(solution)/shard_map/correlate/pallas_call | solution.py:496
  71.9 2.1 %convert_element_type.3 = bf16[2048,128]{1,0:T(8,128)(2,1)} convert(f32[2048,128]{1,0:T(8,128)} %correlate.1) | non-fusion elementwise | flops 262144 | bytes 1572864 | tf_op jit(solution)/shard_map/convert_element_type | solution.py:525

commit v4 on v3

--- a/solution.py
+++ b/solution.py
@@ -92,7 +92,7 @@
             crossed[:, pl.ds(at, 16), si * 128 : (si + 1) * 128] = part
         return carry
 
-    lax.fori_loop(0, groups, step, 0, unroll=16)
+    lax.fori_loop(0, groups, step, 0, unroll=40)
 
 
 class Place:
@@ -316,16 +316,18 @@
         self.copy(self.side, self.after_y, 3, self.place.far(True)).start()
 
     def final(self, out):
+        rest = [self.along_y(si, 0) for si in range(len(self.stage))]
         self.wait(self.after_x, 2)
-        self.wait(self.after_y, 3)
         for si, s in enumerate(self.stage):
             total = self.parts[si, 0, YS - 1, :FIRST].astype(jnp.float32)
             total += self.over_x[si, YS - 1].astype(jnp.float32)
             for turn in range(YS - 1):
                 total += self.after_x[si, turn].astype(jnp.float32)
             out[pl.ds(s, FIRST, stride=VS), :] = total
-            rest = self.along_y(si, 0) + self.after_y[si].astype(jnp.float32)
-            out[pl.ds(FIRST * VS + s, REST, stride=VS), :] = rest
+        self.wait(self.after_y, 3)
+        for si, s in enumerate(self.stage):
+            last = rest[si] + self.after_y[si].astype(jnp.float32)
+            out[pl.ds(FIRST * VS + s, REST, stride=VS), :] = last
 
     def drain(self):
         for ref, sem in ((self.over_x, 0), (self.over_y, 1), (self.after_x, 2), (self.after_y, 3), (self.passing, 4)):
@@ -403,7 +405,7 @@
 )
 
 
-def kernel(spectra, lag_table, pattern, slots, out, rb, turned, wide, crossed, spec, table, load, *rest):
+def kernel(spectra, lag_table, pattern, slots, out, rb, turned, wide, crossed, spec, table, stacked, load, *rest):
     sums, (g_send, g_recv, r_send, r_recv), bufs = rest[:7], rest[7:11], rest[11:]
     loads = []
     for n in range(5):
@@ -474,19 +476,24 @@
         "gather": lambda n: next(steps[n])(),
         "group": group,
         "select": select,
-        "cross": lambda n, piece: cross(rb, wide, crossed, len(STAGES[n]), piece * 16, 16),
+        "cross": lambda n, piece: cross(rb, wide, crossed, len(STAGES[n]), piece * 20, 40) if piece % 2 == 0 and piece < 4 else None,
         "lags": lags,
         "relay": lambda n: reduces[n].relay(),
         "after_x": lambda n: reduces[n].combine_x(),
         "after_y": lambda n: reduces[n].combine_y(),
-        "final": lambda s: reduces[s].final(out),
+        "final": lambda s: reduces[s].final(stacked),
     }
     for name, *arguments in PROGRAM:
         run[name](*arguments)
+    out[...] = stacked[...].astype(jnp.bfloat16)
     for gather in gathers:
         gather.drain()
     for reduce in reduces:
         reduce.drain()
+
+
+def hand_on(source, target):
+    target[...] = source[...]
 
 
 def per_device(spectra, pattern, slot_of_pair, table):
@@ -495,7 +502,7 @@
     hbm = pl.BlockSpec(memory_space=pl.ANY)
     stacks = pl.pallas_call(
         kernel,
-        out_shape=jax.ShapeDtypeStruct((LAGS * VS, 128), jnp.float32),
+        out_shape=jax.ShapeDtypeStruct((LAGS * VS, 128), jnp.bfloat16),
         in_specs=[hbm, hbm, smem, smem],
         out_specs=vmem,
         scratch_shapes=[
@@ -505,6 +512,7 @@
             pltpu.VMEM((SLOTS, 2 * F, 128 * MOST), jnp.bfloat16),
             pltpu.VMEM((2, WINDOWS // 8, F, 128), jnp.bfloat16),
             pltpu.VMEM((LAGS, 2 * F), jnp.bfloat16),
+            pltpu.VMEM((LAGS * VS, 128), jnp.float32),
             pltpu.SemaphoreType.DMA((6,)),
             pltpu.VMEM((VS, 2, YS, LAGS, 128), jnp.bfloat16),
             pltpu.VMEM((VS, YS, FIRST, 128), jnp.bfloat16),
@@ -522,7 +530,14 @@
         compiler_params=pltpu.CompilerParams(collective_id=0, has_side_effects=True, vmem_limit_bytes=56 << 20),
         name="correlate",
     )(spectra, table, pattern, slot_of_pair)
-    return stacks.astype(jnp.bfloat16).reshape(1, LAGS, VS, 128)
+    stacks = pl.pallas_call(
+        hand_on,
+        out_shape=jax.ShapeDtypeStruct(stacks.shape, stacks.dtype),
+        in_specs=[vmem],
+        out_specs=vmem,
+        name="hand_on",
+    )(stacks)
+    return stacks.reshape(1, LAGS, VS, 128)
 
 
 def solution(mesh):

time: 74.3 us -> 72.9 us (0.981); the launches traced: 74 us -> 71.7 us
  other arithmetic: 2.07 us -> 0 us
    pallas_call x1, Pallas kernels: 71.9 us -> 69.8 us  [per_device(): pl.pallas_call(kernel, out_shape=jax.ShapeDtypeStruct((LAGS * VS, 128), j...]
    convert_element_type x1 -> x0, other arithmetic: 2.07 us -> none  [per_device(): return stacks.astype(jnp.bfloat16).reshape(1, LAGS, VS, 128)]
    pallas_call x0 -> x1, Pallas kernels: none -> 1.87 us  [per_device(): pl.pallas_call(hand_on, out_shape=jax.ShapeDtypeStruct(stacks.shape, stac...]
where the time goes in v4:
time: 72.9 us; the launch traced here: 71.7 us
  Pallas kernels  71.6 us (98%)
    pallas_call x1, Pallas kernels, per_device(): pl.pallas_call(kernel, out_shape=jax.ShapeDtypeStruct((LAGS * VS, 128), j...  69.8 us
    pallas_call x1, Pallas kernels, per_device(): pl.pallas_call(hand_on, out_shape=jax.ShapeDtypeStruct(stacks.shape, stac...  1.87 us

profile of v4, /device:TPU:1, one launch (start us, length us, event | category | flops | bytes accessed | tf_op | source)
XLA Modules:
  0.0 71.7 jit_solution(5394523295859889632)
XLA Ops:
  0.0 69.8 %correlate.1.source = bf16[2048,128]{1,0:T(8,128)(2,1)} custom-call(bf16[2,16,640,128]{3,2,1,0:T(8,128)(2,1)} %spectra.1, bf16[512,1280]{1,0:T(8,128)(2,1)} %constant.2.clone.lag_table, s32[32,32]{1,0:T(8,128)} %pattern.1, s32[32,32]{1,0:T(8,128)} %slots.1), custom_call_target="tpu_custom_call" | custom-call | tf_op jit(solution)/shard_map/correlate/pallas_call | solution.py:503
  69.8 1.9 %hand_on.1 = bf16[2048,128]{1,0:T(8,128)(2,1)} custom-call(bf16[2048,128]{1,0:T(8,128)(2,1)} %correlate.1.source), custom_call_target="tpu_custom_call" | custom-call | tf_op jit(solution)/shard_map/hand_on/pallas_call | solution.py:533

commit v5 on v4

--- a/solution.py
+++ b/solution.py
@@ -485,7 +485,7 @@
     }
     for name, *arguments in PROGRAM:
         run[name](*arguments)
-    out[...] = stacked[...].astype(jnp.bfloat16)
+    out[...] = stacked[: LAGS * VS, :].astype(jnp.bfloat16)
     for gather in gathers:
         gather.drain()
     for reduce in reduces:
@@ -512,7 +512,7 @@
             pltpu.VMEM((SLOTS, 2 * F, 128 * MOST), jnp.bfloat16),
             pltpu.VMEM((2, WINDOWS // 8, F, 128), jnp.bfloat16),
             pltpu.VMEM((LAGS, 2 * F), jnp.bfloat16),
-            pltpu.VMEM((LAGS * VS, 128), jnp.float32),
+            pltpu.VMEM((LAGS * VS + 8, 128), jnp.float32),
             pltpu.SemaphoreType.DMA((6,)),
             pltpu.VMEM((VS, 2, YS, LAGS, 128), jnp.bfloat16),
             pltpu.VMEM((VS, YS, FIRST, 128), jnp.bfloat16),

time: 72.9 us -> 72.9 us (level)
  no operation moved by 1% of the time
where the time goes in v5:
time: 72.9 us; the launch traced here: 71.7 us
  Pallas kernels  71.6 us (98%)
    pallas_call x1, Pallas kernels, per_device(): pl.pallas_call(kernel, out_shape=jax.ShapeDtypeStruct((LAGS * VS, 128), j...  69.8 us
    pallas_call x1, Pallas kernels, per_device(): pl.pallas_call(hand_on, out_shape=jax.ShapeDtypeStruct(stacks.shape, stac...  1.87 us

profile of v5, /device:TPU:1, one launch (start us, length us, event | category | flops | bytes accessed | tf_op | source)
XLA Modules:
  0.0 71.7 jit_solution(3793034956018039898)
XLA Ops:
  0.0 69.8 %correlate.1.source = bf16[2048,128]{1,0:T(8,128)(2,1)} custom-call(bf16[2,16,640,128]{3,2,1,0:T(8,128)(2,1)} %spectra.1, bf16[512,1280]{1,0:T(8,128)(2,1)} %constant.2.clone.lag_table, s32[32,32]{1,0:T(8,128)} %pattern.1, s32[32,32]{1,0:T(8,128)} %slots.1), custom_call_target="tpu_custom_call" | custom-call | tf_op jit(solution)/shard_map/correlate/pallas_call | solution.py:503
  69.8 1.9 %hand_on.1 = bf16[2048,128]{1,0:T(8,128)(2,1)} custom-call(bf16[2048,128]{1,0:T(8,128)(2,1)} %correlate.1.source), custom_call_target="tpu_custom_call" | custom-call | tf_op jit(solution)/shard_map/hand_on/pallas_call | solution.py:533
